TPU v7x, 128 devices: a whole 4x4x4 slice. The times are simulated.
128 devices in a mesh: slab: 32 (over y, z, x_lo), run: 4 (over x_hi, core).
Axes of the slice: x: 4 (x_hi: 2, x_lo: 2; x = x_hi * 2 + x_lo), y: 4, z: 4, core: 2. Of those that a mesh axis runs over, the one named last changes fastest.
Arguments:
- material: int32 [128, 256, 256], P('slab'), may hold values from 0 to 15
- eps_table: float32 [16], replicated, may hold values from 1 to 12
- surface_mask: int32 [128], P('slab'), may hold values 0 or 1
- excite_map: int32 [4], P('run'), may hold values from 0 to 3
- mode_profiles: float32 [4, 256, 256], P(None, 'slab'), may hold values from -4 to 4
- port_eps: float32 [256, 256], P('slab'), may hold values from 1 to 4
- cotangent: float32 [4, 128, 256, 256], P('run', 'slab'), may hold values from -6 to 6
Outputs:
- gradient: float32 [128, 256, 256], P('slab')
- field_out: float32 [4, 128, 256, 256], P('run', 'slab')
Inputs may be any that keep to these rules, and one draw needn't show every extreme that they name: material indices into the permittivity table. `surface_mask`: 0 or 1 for each x layer. `excite_map`: an index of a mode profile.
All inputs are finite; a program needn't handle non-finite values. No bound on the sum of `surface_mask` on one device may be relied on, other than what follows from the above.
Results may differ from a plain program's by a relative error of at most 0.0001.
Values sent between devices are 32-bit elements; how exact they have to be, the bound alone decides.
A program may use at most 128 MiB of HBM per device.

v0:
```python
import jax
import jax.numpy as jnp
from jax import lax
from jax.sharding import PartitionSpec as P

STEPS = 6
time_step = 0.5


def padded_2(x, sides, width):
    for axis, dim in sides:
        size, length = (lax.axis_size(axis), x.shape[dim])
        up = [(i, (i + 1) % size) for i in range(size - 1)]
        down = [(j, i) for i, j in up]
        last = lax.slice_in_dim(x, length - width, length, axis=dim)
        first = lax.slice_in_dim(x, 0, width, axis=dim)
        before = lax.ppermute(last, axis, up)
        after = lax.ppermute(first, axis, down)
        x = jnp.concatenate([before, x, after], axis=dim)
    return x


def passed_along(block, axis, distance):
    devices = range(lax.axis_size(axis))
    route = [(i - distance, i) for i in devices if i - distance in devices]
    return lax.ppermute(block, axis, route)


def rim_zero(field, along):
    return jnp.zeros_like(lax.slice_in_dim(field, 0, 1, axis=along))


def ahead(field, along, border):
    length = field.shape[along]
    return jnp.concatenate([lax.slice_in_dim(field, 1, length, axis=along), border], along) - field


def behind(field, along, border):
    length = field.shape[along]
    return field - jnp.concatenate(
        [border, lax.slice_in_dim(field, 0, length - 1, axis=along)], along
    )


def update_magnetic(electric, magnetic, upper_y, upper_z):
    electric_x, electric_y, electric_z = electric
    magnetic_x, magnetic_y, magnetic_z = magnetic
    magnetic_x = magnetic_x - time_step * (
        ahead(electric_z, 2, rim_zero(electric_z, 2))
        - ahead(electric_y, 3, rim_zero(electric_y, 3))
    )
    magnetic_y = magnetic_y - time_step * (
        ahead(electric_x, 3, rim_zero(electric_x, 3)) - ahead(electric_z, 1, upper_z)
    )
    magnetic_z = magnetic_z - time_step * (
        ahead(electric_y, 1, upper_y) - ahead(electric_x, 2, rim_zero(electric_x, 2))
    )
    return (magnetic_x, magnetic_y, magnetic_z)


def update_electric(electric, magnetic, lower_y, lower_z, coefficient, source_y, source_z):
    electric_x, electric_y, electric_z = electric
    magnetic_x, magnetic_y, magnetic_z = magnetic
    electric_x = electric_x + coefficient * (
        behind(magnetic_z, 2, rim_zero(magnetic_z, 2))
        - behind(magnetic_y, 3, rim_zero(magnetic_y, 3))
    )
    electric_y = (
        electric_y
        + coefficient
        * (behind(magnetic_x, 3, rim_zero(magnetic_x, 3)) - behind(magnetic_z, 1, lower_z))
        + source_y
    )
    electric_z = (
        electric_z
        + coefficient
        * (behind(magnetic_y, 1, lower_y) - behind(magnetic_x, 2, rim_zero(magnetic_x, 2)))
        + source_z
    )
    return (electric_x, electric_y, electric_z)


def modal_advance(modal_now, modal_old, padded, port_coefficient, profile, forcing):
    middle = padded[1:-1]
    zpadded = jnp.pad(middle, ((0, 0), (1, 1)))
    laplacian = padded[2:] + padded[:-2] + zpadded[:, 2:] + zpadded[:, :-2] - 4.0 * middle
    return 2.0 * modal_now - modal_old + port_coefficient * laplacian + forcing * profile


def forcing_at(counter):
    moment = (counter + 1).astype(jnp.float32)
    return 2.0 * jnp.sin(0.3 * moment) * (1.0 - jnp.exp(-0.5 * moment))


def permittivity_of(material, eps_table):
    levels = jnp.arange(eps_table.shape[0], dtype=jnp.int32)
    picked = (material[None] == levels[:, None, None, None]).astype(jnp.float32)
    return jnp.sum(picked * eps_table[:, None, None, None], axis=0)


def local(material, eps_table, surface_mask, excite_map, mode_profiles, port_eps, cotangent):
    coefficient = time_step / permittivity_of(material, eps_table)
    mask_column = surface_mask.astype(jnp.float32)[:, None, None]
    injection = 0.25 * coefficient * mask_column
    selector = jnp.array([1.0, 0.0], jnp.float32)[:, None, None, None]
    choose = (jnp.arange(mode_profiles.shape[0], dtype=jnp.int32) == excite_map[0]).astype(
        jnp.float32
    )
    profile = jnp.sum(mode_profiles * choose[:, None, None], axis=0)
    port_coefficient = 0.25 / port_eps

    def port_step(modal_now, modal_old, forcing):
        padded = padded_2(modal_now, (("slab", 0),), 1)
        modal_next = modal_advance(modal_now, modal_old, padded, port_coefficient, profile, forcing)
        incident_e, incident_h = (
            lax.all_gather(modal_next, "slab", axis=0, tiled=True),
            lax.all_gather(modal_next - modal_now, "slab", axis=0, tiled=True),
        )
        return (modal_next, incident_e, incident_h)

    zeros = jnp.zeros((2,) + coefficient.shape, jnp.float32)
    electric = (zeros.at[0].set(cotangent[0]), zeros, zeros.at[1].set(cotangent[0]))
    magnetic = (zeros, zeros, zeros)
    modal_zero = jnp.zeros_like(profile)

    def advance(counter, carried):
        electric, magnetic, modal_now, modal_old, gradient_sum = carried
        modal_next, incident_e, incident_h = port_step(modal_now, modal_old, forcing_at(counter))
        electric_x, electric_y, electric_z = electric
        upper_rim = passed_along(
            jnp.concatenate([electric_y[:, 0:1], electric_z[:, 0:1]], 1), "slab", -1
        )
        magnetic = update_magnetic(electric, magnetic, upper_rim[:, 0:1], upper_rim[:, 1:2])
        lower_rim = passed_along(
            jnp.concatenate([magnetic[1][:, -1:], magnetic[2][:, -1:]], 1), "slab", 1
        )
        lower_y = lower_rim[:, 0:1]
        lower_z = lower_rim[:, 1:2]
        electric = update_electric(
            electric,
            magnetic,
            lower_y,
            lower_z,
            coefficient,
            selector * (injection * incident_h),
            selector * (injection * incident_e),
        )
        gradient_sum = gradient_sum + (
            electric[0][0] * electric[0][1]
            + electric[1][0] * electric[1][1]
            + electric[2][0] * electric[2][1]
        )
        return (electric, magnetic, modal_next, modal_now, gradient_sum)

    carried = lax.fori_loop(
        0,
        STEPS,
        advance,
        (electric, magnetic, modal_zero, modal_zero, jnp.zeros(coefficient.shape, jnp.float32)),
    )
    gradient = lax.psum(carried[4], "run")
    return (gradient, carried[0][1][0][None])


def solution(mesh):
    in_specs = (
        P("slab", None, None),
        P(),
        P("slab"),
        P("run"),
        P(None, "slab", None),
        P("slab", None),
        P("run", "slab", None, None),
    )
    out_specs = (P("slab", None, None), P("run", "slab", None, None))
    return jax.shard_map(local, mesh=mesh, in_specs=in_specs, out_specs=out_specs, check_vma=False)
```

profile of v0, /device:TPU:1, one launch (start us, length us, event | category | flops | bytes accessed | tf_op | source)
XLA Modules:
  0.0 1372.4 jit_solution(14720914317729965856)
XLA Ops:
  14.8 1125.8 %while.35 = (s32[]{:T(128)}, f32[2,4,256,256]{3,2,1,0:T(8,128)S(1)}, f32[2,4,256,256]{3,2,1,0:T(8,128)}, f32[2,4,256,256]{3,2,1,0:T(8,128)}, f32[2,4,256,256]{3,...) while((s32[]{:T(128)}, ...), condition=%wide.region_3.0_spmd.clone.clone, body=%wide.region_2.0_spmd.clone.clone.sunk | while | flops 25982984 | bytes 269106240 | solution.py:155
  20.4 23.2 %collective-permute-done = f32[2,2,256,256]{3,2,1,0:T(8,128)S(1)} collective-permute-done((f32[2,2,256,256]{3,2,1,0:T(8,128)S(1)}, f32[2,2,256,256]{3,2,1,0:T(8,128)S(1)}, u32[]{:S(2)}, u32[]{:S(2)}) %collective-permute-start) | collective-permute-done | bytes 1048608 | tf_op jit(solution)/shard_map/while/body/eval_jaxpr/ppermute | solution.py:26
  48.2 5.4 collective-permute-start.1
  56.7 17.1 %collective-permute-done.2 = f32[1,256]{1,0:T(1,128)S(1)} collective-permute-done((f32[1,256]{1,0:T(1,128)S(1)}, f32[1,256]{1,0:T(1,128)S(1)}, u32[]{:S(2)}, u32[]{:S(2)}) %collective-permute-start.2) | collective-permute-done | bytes 1056 | tf_op jit(solution)/shard_map/while/body/eval_jaxpr/ppermute | solution.py:17
  75.6 69.1 %all_gather.26 = f32[256,256]{1,0:T(8,128)S(1)} all-gather(f32[8,256]{1,0:T(8,128)S(1)} %get-tuple-element.732), channel_id=1, replica_groups=mesh['slab'=32,'run'=4] {'slab'}, dimensions={0}, use_global_device_ids=true | all-gather | bytes 270336 | tf_op jit(solution)/shard_map/while/body/eval_jaxpr/all_gather | solution.py:116
  144.7 63.4 %all_gather.27 = f32[256,256]{1,0:T(8,128)S(1)} all-gather(f32[8,256]{1,0:T(8,128)S(1)} %get-tuple-element.676), channel_id=1, replica_groups=mesh['slab'=32,'run'=4] {'slab'}, dimensions={0}, use_global_device_ids=true | all-gather | bytes 270336 | tf_op jit(solution)/shard_map/while/body/eval_jaxpr/all_gather | solution.py:117
  213.1 5.3 fusion.43
  226.3 12.8 collective-permute-done
  251.5 8.3 collective-permute-done.2
  263.2 63.8 %all_gather.26 = f32[256,256]{1,0:T(8,128)S(1)} all-gather(f32[8,256]{1,0:T(8,128)S(1)} %get-tuple-element.732), channel_id=1, replica_groups=mesh['slab'=32,'run'=4] {'slab'}, dimensions={0}, use_global_device_ids=true | all-gather | bytes 270336 | tf_op jit(solution)/shard_map/while/body/eval_jaxpr/all_gather | solution.py:116
  327.0 65.1 %all_gather.27 = f32[256,256]{1,0:T(8,128)S(1)} all-gather(f32[8,256]{1,0:T(8,128)S(1)} %get-tuple-element.676), channel_id=1, replica_groups=mesh['slab'=32,'run'=4] {'slab'}, dimensions={0}, use_global_device_ids=true | all-gather | bytes 270336 | tf_op jit(solution)/shard_map/while/body/eval_jaxpr/all_gather | solution.py:117
  397.1 5.3 fusion.43
  411.6 12.7 collective-permute-done
  435.3 8.9 collective-permute-done.2
  445.4 65.4 %all_gather.26 = f32[256,256]{1,0:T(8,128)S(1)} all-gather(f32[8,256]{1,0:T(8,128)S(1)} %get-tuple-element.732), channel_id=1, replica_groups=mesh['slab'=32,'run'=4] {'slab'}, dimensions={0}, use_global_device_ids=true | all-gather | bytes 270336 | tf_op jit(solution)/shard_map/while/body/eval_jaxpr/all_gather | solution.py:116
  510.8 63.5 %all_gather.27 = f32[256,256]{1,0:T(8,128)S(1)} all-gather(f32[8,256]{1,0:T(8,128)S(1)} %get-tuple-element.676), channel_id=1, replica_groups=mesh['slab'=32,'run'=4] {'slab'}, dimensions={0}, use_global_device_ids=true | all-gather | bytes 270336 | tf_op jit(solution)/shard_map/while/body/eval_jaxpr/all_gather | solution.py:117
  579.3 5.3 fusion.43
  593.8 13.2 collective-permute-done
  619.5 8.9 collective-permute-done.2
  629.2 65.6 %all_gather.26 = f32[256,256]{1,0:T(8,128)S(1)} all-gather(f32[8,256]{1,0:T(8,128)S(1)} %get-tuple-element.732), channel_id=1, replica_groups=mesh['slab'=32,'run'=4] {'slab'}, dimensions={0}, use_global_device_ids=true | all-gather | bytes 270336 | tf_op jit(solution)/shard_map/while/body/eval_jaxpr/all_gather | solution.py:116
  694.9 64.3 %all_gather.27 = f32[256,256]{1,0:T(8,128)S(1)} all-gather(f32[8,256]{1,0:T(8,128)S(1)} %get-tuple-element.676), channel_id=1, replica_groups=mesh['slab'=32,'run'=4] {'slab'}, dimensions={0}, use_global_device_ids=true | all-gather | bytes 270336 | tf_op jit(solution)/shard_map/while/body/eval_jaxpr/all_gather | solution.py:117
  764.2 5.3 fusion.43
  778.7 13.0 collective-permute-done
  803.7 8.7 collective-permute-done.2
  813.4 65.3 %all_gather.26 = f32[256,256]{1,0:T(8,128)S(1)} all-gather(f32[8,256]{1,0:T(8,128)S(1)} %get-tuple-element.732), channel_id=1, replica_groups=mesh['slab'=32,'run'=4] {'slab'}, dimensions={0}, use_global_device_ids=true | all-gather | bytes 270336 | tf_op jit(solution)/shard_map/while/body/eval_jaxpr/all_gather | solution.py:116
  878.8 64.0 %all_gather.27 = f32[256,256]{1,0:T(8,128)S(1)} all-gather(f32[8,256]{1,0:T(8,128)S(1)} %get-tuple-element.676), channel_id=1, replica_groups=mesh['slab'=32,'run'=4] {'slab'}, dimensions={0}, use_global_device_ids=true | all-gather | bytes 270336 | tf_op jit(solution)/shard_map/while/body/eval_jaxpr/all_gather | solution.py:117
  962.3 12.9 collective-permute-done
  987.6 8.8 collective-permute-done.2
  997.6 65.0 %all_gather.26 = f32[256,256]{1,0:T(8,128)S(1)} all-gather(f32[8,256]{1,0:T(8,128)S(1)} %get-tuple-element.732), channel_id=1, replica_groups=mesh['slab'=32,'run'=4] {'slab'}, dimensions={0}, use_global_device_ids=true | all-gather | bytes 270336 | tf_op jit(solution)/shard_map/while/body/eval_jaxpr/all_gather | solution.py:116
  1062.7 63.9 %all_gather.27 = f32[256,256]{1,0:T(8,128)S(1)} all-gather(f32[8,256]{1,0:T(8,128)S(1)} %get-tuple-element.676), channel_id=1, replica_groups=mesh['slab'=32,'run'=4] {'slab'}, dimensions={0}, use_global_device_ids=true | all-gather | bytes 270336 | tf_op jit(solution)/shard_map/while/body/eval_jaxpr/all_gather | solution.py:117
  1131.6 5.3 fusion.43
  1142.9 220.3 %all-reduce.13.cloned.1.call-done = f32[4,256,256]{2,1,0:T(8,128)} async-done(((f32[4,256,256]{2,1,0:T(8,128)}), f32[4,256,256]{2,1,0:T(8,128)}) %all-reduce.13.cloned.1.call-update) | async-done | bytes 1048592 | tf_op jit(solution)/shard_map/psum | solution.py:161
  (468 shorter events, 175.4 us)
Async XLA Ops:
  7.2 1356.1 %all-reduce.13.cloned.1.call-start = ((), (), s32[]{:S(2)}) async-start(), calls=%async_computation | async-start | bytes 2097152 | tf_op jit(solution)/shard_map/psum | solution.py:161
  14.8 60.2 %copy-start.17 = (f32[8,256]{1,0:T(8,128)}, f32[8,256]{1,0:T(8,128)S(1)}, u32[]{:S(2)}) copy-start(f32[8,256]{1,0:T(8,128)S(1)} %get-tuple-element.736) | copy-start | bytes 24580 | tf_op jit(solution)/shard_map/while
  17.2 26.3 %collective-permute-start = (f32[2,2,256,256]{3,2,1,0:T(8,128)S(1)}, f32[2,2,256,256]{3,2,1,0:T(8,128)S(1)}, u32[]{:S(2)}, u32[]{:S(2)}) collective-permute-start(f32[2,2,256,256]{3,2,1,0:T(8,128)S(1)} %pad_maximum_fusion.6), channel_id=1, source_target_pairs={{4,0},{8,4},{12,8},{16,12},{20,16},{24,20},{28,24},{32,28},{36,32}... | collective-permute-start | bytes 3145736 | tf_op jit(solution)/shard_map/while/body/eval_jaxpr/ppermute | solution.py:26
  48.2 162.0 %collective-permute-start.1 = (f32[2,2,256,256]{3,2,1,0:T(8,128)}, f32[2,2,256,256]{3,2,1,0:T(8,128)}, u32[]{:S(2)}, u32[]{:S(2)}) collective-permute-start(f32[2,2,256,256]{3,2,1,0:T(8,128)} %pad_maximum_fusion.7), channel_id=1, source_target_pairs={{0,4},{4,8},{8,12},{12,16},{16,20},{20,24},{24,28},{28,32},{32,36}... | collective-permute-start | bytes 3145736 | tf_op jit(solution)/shard_map/while/body/eval_jaxpr/ppermute | solution.py:26
  53.6 20.2 %collective-permute-start.2 = (f32[1,256]{1,0:T(1,128)S(1)}, f32[1,256]{1,0:T(1,128)S(1)}, u32[]{:S(2)}, u32[]{:S(2)}) collective-permute-start(f32[1,256]{1,0:T(1,128)S(1)} %get-tuple-element.673), channel_id=1, source_target_pairs={{0,4},{4,8},{8,12},{12,16},{16,20},{20,24},{24,28},{28,32},{32,36}... | collective-permute-start | bytes 3080 | tf_op jit(solution)/shard_map/while/body/eval_jaxpr/ppermute | solution.py:17
  55.3 19.6 %collective-permute-start.3 = (f32[1,256]{1,0:T(1,128)S(1)}, f32[1,256]{1,0:T(1,128)S(1)}, u32[]{:S(2)}, u32[]{:S(2)}) collective-permute-start(f32[1,256]{1,0:T(1,128)S(1)} %get-tuple-element.674), channel_id=1, source_target_pairs={{4,0},{8,4},{12,8},{16,12},{20,16},{24,20},{28,24},{32,28},{36,32}... | collective-permute-start | bytes 3080 | tf_op jit(solution)/shard_map/while/body/eval_jaxpr/ppermute | solution.py:18
  75.6 134.0 %copy-start.11 = (f32[2,4,256,256]{3,2,1,0:T(8,128)S(1)}, f32[2,4,256,256]{3,2,1,0:T(8,128)}, u32[]{:S(2)}) copy-start(f32[2,4,256,256]{3,2,1,0:T(8,128)} %copy-done.10) | copy-start | bytes 6291460 | tf_op jit(solution)/shard_map/while
  223.1 16.0 %collective-permute-start = (f32[2,2,256,256]{3,2,1,0:T(8,128)S(1)}, f32[2,2,256,256]{3,2,1,0:T(8,128)S(1)}, u32[]{:S(2)}, u32[]{:S(2)}) collective-permute-start(f32[2,2,256,256]{3,2,1,0:T(8,128)S(1)} %pad_maximum_fusion.6), channel_id=1, source_target_pairs={{4,0},{8,4},{12,8},{16,12},{20,16},{24,20},{28,24},{32,28},{36,32}... | collective-permute-start | bytes 3145736 | tf_op jit(solution)/shard_map/while/body/eval_jaxpr/ppermute | solution.py:26
  243.7 150.5 %collective-permute-start.1 = (f32[2,2,256,256]{3,2,1,0:T(8,128)}, f32[2,2,256,256]{3,2,1,0:T(8,128)}, u32[]{:S(2)}, u32[]{:S(2)}) collective-permute-start(f32[2,2,256,256]{3,2,1,0:T(8,128)} %pad_maximum_fusion.7), channel_id=1, source_target_pairs={{0,4},{4,8},{8,12},{12,16},{16,20},{20,24},{24,28},{28,32},{32,36}... | collective-permute-start | bytes 3145736 | tf_op jit(solution)/shard_map/while/body/eval_jaxpr/ppermute | solution.py:26
  248.8 11.1 collective-permute-start.2
  250.1 12.5 collective-permute-start.3
  263.2 130.5 %copy-start.11 = (f32[2,4,256,256]{3,2,1,0:T(8,128)S(1)}, f32[2,4,256,256]{3,2,1,0:T(8,128)}, u32[]{:S(2)}) copy-start(f32[2,4,256,256]{3,2,1,0:T(8,128)} %copy-done.10) | copy-start | bytes 6291460 | tf_op jit(solution)/shard_map/while
  408.5 15.9 %collective-permute-start = (f32[2,2,256,256]{3,2,1,0:T(8,128)S(1)}, f32[2,2,256,256]{3,2,1,0:T(8,128)S(1)}, u32[]{:S(2)}, u32[]{:S(2)}) collective-permute-start(f32[2,2,256,256]{3,2,1,0:T(8,128)S(1)} %pad_maximum_fusion.6), channel_id=1, source_target_pairs={{4,0},{8,4},{12,8},{16,12},{20,16},{24,20},{28,24},{32,28},{36,32}... | collective-permute-start | bytes 3145736 | tf_op jit(solution)/shard_map/while/body/eval_jaxpr/ppermute | solution.py:26
  429.0 147.4 %collective-permute-start.1 = (f32[2,2,256,256]{3,2,1,0:T(8,128)}, f32[2,2,256,256]{3,2,1,0:T(8,128)}, u32[]{:S(2)}, u32[]{:S(2)}) collective-permute-start(f32[2,2,256,256]{3,2,1,0:T(8,128)} %pad_maximum_fusion.7), channel_id=1, source_target_pairs={{0,4},{4,8},{8,12},{12,16},{16,20},{20,24},{24,28},{28,32},{32,36}... | collective-permute-start | bytes 3145736 | tf_op jit(solution)/shard_map/while/body/eval_jaxpr/ppermute | solution.py:26
  432.6 11.6 collective-permute-start.2
  433.9 10.8 collective-permute-start.3
  445.4 130.4 %copy-start.11 = (f32[2,4,256,256]{3,2,1,0:T(8,128)S(1)}, f32[2,4,256,256]{3,2,1,0:T(8,128)}, u32[]{:S(2)}) copy-start(f32[2,4,256,256]{3,2,1,0:T(8,128)} %copy-done.10) | copy-start | bytes 6291460 | tf_op jit(solution)/shard_map/while
  590.6 16.4 %collective-permute-start = (f32[2,2,256,256]{3,2,1,0:T(8,128)S(1)}, f32[2,2,256,256]{3,2,1,0:T(8,128)S(1)}, u32[]{:S(2)}, u32[]{:S(2)}) collective-permute-start(f32[2,2,256,256]{3,2,1,0:T(8,128)S(1)} %pad_maximum_fusion.6), channel_id=1, source_target_pairs={{4,0},{8,4},{12,8},{16,12},{20,16},{24,20},{28,24},{32,28},{36,32}... | collective-permute-start | bytes 3145736 | tf_op jit(solution)/shard_map/while/body/eval_jaxpr/ppermute | solution.py:26
  611.6 149.6 %collective-permute-start.1 = (f32[2,2,256,256]{3,2,1,0:T(8,128)}, f32[2,2,256,256]{3,2,1,0:T(8,128)}, u32[]{:S(2)}, u32[]{:S(2)}) collective-permute-start(f32[2,2,256,256]{3,2,1,0:T(8,128)} %pad_maximum_fusion.7), channel_id=1, source_target_pairs={{0,4},{4,8},{8,12},{12,16},{16,20},{20,24},{24,28},{28,32},{32,36}... | collective-permute-start | bytes 3145736 | tf_op jit(solution)/shard_map/while/body/eval_jaxpr/ppermute | solution.py:26
  616.8 11.6 collective-permute-start.2
  618.1 10.5 collective-permute-start.3
  629.2 131.5 %copy-start.11 = (f32[2,4,256,256]{3,2,1,0:T(8,128)S(1)}, f32[2,4,256,256]{3,2,1,0:T(8,128)}, u32[]{:S(2)}) copy-start(f32[2,4,256,256]{3,2,1,0:T(8,128)} %copy-done.10) | copy-start | bytes 6291460 | tf_op jit(solution)/shard_map/while
  775.5 16.2 %collective-permute-start = (f32[2,2,256,256]{3,2,1,0:T(8,128)S(1)}, f32[2,2,256,256]{3,2,1,0:T(8,128)S(1)}, u32[]{:S(2)}, u32[]{:S(2)}) collective-permute-start(f32[2,2,256,256]{3,2,1,0:T(8,128)S(1)} %pad_maximum_fusion.6), channel_id=1, source_target_pairs={{4,0},{8,4},{12,8},{16,12},{20,16},{24,20},{28,24},{32,28},{36,32}... | collective-permute-start | bytes 3145736 | tf_op jit(solution)/shard_map/while/body/eval_jaxpr/ppermute | solution.py:26
  796.4 148.5 %collective-permute-start.1 = (f32[2,2,256,256]{3,2,1,0:T(8,128)}, f32[2,2,256,256]{3,2,1,0:T(8,128)}, u32[]{:S(2)}, u32[]{:S(2)}) collective-permute-start(f32[2,2,256,256]{3,2,1,0:T(8,128)} %pad_maximum_fusion.7), channel_id=1, source_target_pairs={{0,4},{4,8},{8,12},{12,16},{16,20},{20,24},{24,28},{28,32},{32,36}... | collective-permute-start | bytes 3145736 | tf_op jit(solution)/shard_map/while/body/eval_jaxpr/ppermute | solution.py:26
  801.0 11.4 collective-permute-start.2
  802.3 10.5 collective-permute-start.3
  813.4 130.9 %copy-start.11 = (f32[2,4,256,256]{3,2,1,0:T(8,128)S(1)}, f32[2,4,256,256]{3,2,1,0:T(8,128)}, u32[]{:S(2)}) copy-start(f32[2,4,256,256]{3,2,1,0:T(8,128)} %copy-done.10) | copy-start | bytes 6291460 | tf_op jit(solution)/shard_map/while
  959.1 16.1 %collective-permute-start = (f32[2,2,256,256]{3,2,1,0:T(8,128)S(1)}, f32[2,2,256,256]{3,2,1,0:T(8,128)S(1)}, u32[]{:S(2)}, u32[]{:S(2)}) collective-permute-start(f32[2,2,256,256]{3,2,1,0:T(8,128)S(1)} %pad_maximum_fusion.6), channel_id=1, source_target_pairs={{4,0},{8,4},{12,8},{16,12},{20,16},{24,20},{28,24},{32,28},{36,32}... | collective-permute-start | bytes 3145736 | tf_op jit(solution)/shard_map/while/body/eval_jaxpr/ppermute | solution.py:26
  979.8 148.9 %collective-permute-start.1 = (f32[2,2,256,256]{3,2,1,0:T(8,128)}, f32[2,2,256,256]{3,2,1,0:T(8,128)}, u32[]{:S(2)}, u32[]{:S(2)}) collective-permute-start(f32[2,2,256,256]{3,2,1,0:T(8,128)} %pad_maximum_fusion.7), channel_id=1, source_target_pairs={{0,4},{4,8},{8,12},{12,16},{16,20},{20,24},{24,28},{28,32},{32,36}... | collective-permute-start | bytes 3145736 | tf_op jit(solution)/shard_map/while/body/eval_jaxpr/ppermute | solution.py:26
  984.9 11.6 collective-permute-start.2
  986.2 10.8 collective-permute-start.3
  997.6 130.5 %copy-start.11 = (f32[2,4,256,256]{3,2,1,0:T(8,128)S(1)}, f32[2,4,256,256]{3,2,1,0:T(8,128)}, u32[]{:S(2)}) copy-start(f32[2,4,256,256]{3,2,1,0:T(8,128)} %copy-done.10) | copy-start | bytes 6291460 | tf_op jit(solution)/shard_map/while
  (131 other events, 1198.9 us)
Sparse Core Ops, SparseCore 0:
  1140.7 222.4 all-reduce.12
where the time goes:
time: 1370 us
  blocking collectives  778 us (57%)
  waiting for transfers between devices  374 us (27%)
  other arithmetic  95.8 us (7%)
  local copies, waits for them, and re-layouts  53.6 us (4%)
  starting transfers between devices  52.5 us (4%)
  between operations  14.8 us (1%)
    all_gather x6, blocking collectives, port_step(): lax.all_gather(modal_next, 'slab', axis=0, tiled=True)  394 us
    all_gather x6, blocking collectives, port_step(): lax.all_gather(modal_next - modal_now, 'slab', axis=0, tiled=True)  384 us
    psum x1, waiting for transfers between devices, local(): gradient = lax.psum(carried[4], 'run')  220 us
    ppermute x12, waiting for transfers between devices, passed_along(): return lax.ppermute(block, axis, route)  87.8 us
    ppermute x6, waiting for transfers between devices, padded_2(): before = lax.ppermute(last, axis, up)  60.7 us
    ppermute x12, starting transfers between devices, passed_along(): return lax.ppermute(block, axis, route)  36.6 us
    add x6, other arithmetic, update_electric(): electric_z + coefficient * (behind(magnetic_y, 1, lower_y) - behind(magne...  31.7 us
  transfers between devices with their start and end apart: 25, of which 19 were waited for; matrix products, arithmetic and copies ran while one was open for 2% of the time, Pallas kernels for 0%

commit v1 on v0

--- a/solution.py
+++ b/solution.py
@@ -5,6 +5,13 @@
 
 STEPS = 6
 time_step = 0.5
+
+
+def all_by_exchange(value, axis, d):
+    size = lax.axis_size(axis)
+    pieces = jnp.stack([value for _ in range(size)])
+    pieces = lax.all_to_all(pieces, axis, split_axis=0, concat_axis=0)
+    return jnp.concatenate(pieces, axis=d)
 
 
 def padded_2(x, sides, width):
@@ -113,7 +120,7 @@
         padded = padded_2(modal_now, (("slab", 0),), 1)
         modal_next = modal_advance(modal_now, modal_old, padded, port_coefficient, profile, forcing)
         incident_e, incident_h = (
-            lax.all_gather(modal_next, "slab", axis=0, tiled=True),
+            all_by_exchange(modal_next, "slab", 0),
             lax.all_gather(modal_next - modal_now, "slab", axis=0, tiled=True),
         )
         return (modal_next, incident_e, incident_h)

time: 1370 us -> 995 us (0.73)
  blocking collectives: 778 us -> 445 us
  waiting for transfers between devices: 374 us -> 301 us
  starting transfers between devices: 52.5 us -> 71.6 us
    all_gather x6 -> x0, blocking collectives: 394 us -> none  [port_step(): lax.all_gather(modal_next, 'slab', axis=0, tiled=True)]
    psum x1, waiting for transfers between devices: 220 us -> 140 us  [local(): gradient = lax.psum(carried[4], 'run')]
    all_gather x6, blocking collectives: 384 us -> 445 us  [port_step(): lax.all_gather(modal_next - modal_now, 'slab', axis=0, tiled=True)]
    all_to_all x0 -> x6, starting transfers between devices: none -> 30.9 us  [all_by_exchange(): pieces = lax.all_to_all(pieces, axis, split_axis=0, concat_axis=0)]
  transfers between devices with their start and end apart: 25 -> 31, of which waited for: 19 -> 19; matrix products, arithmetic and copies ran while one was open for 2% -> 3% of each run, Pallas kernels for 0% -> 0%
where the time goes in v1:
time: 995 us; the launch traced here: 993 us
  blocking collectives  445 us (45%)
  waiting for transfers between devices  301 us (30%)
  other arithmetic  96.6 us (10%)
  starting transfers between devices  71.6 us (7%)
  local copies, waits for them, and re-layouts  61.1 us (6%)
  between operations  14.8 us (1%)
    all_gather x6, blocking collectives, port_step(): lax.all_gather(modal_next - modal_now, 'slab', axis=0, tiled=True)  445 us
    psum x1, waiting for transfers between devices, local(): gradient = lax.psum(carried[4], 'run')  140 us
    ppermute x12, waiting for transfers between devices, passed_along(): return lax.ppermute(block, axis, route)  87.7 us
    ppermute x6, waiting for transfers between devices, padded_2(): before = lax.ppermute(last, axis, up)  59.7 us
    add x6, other arithmetic, update_electric(): electric_z + coefficient * (behind(magnetic_y, 1, lower_y) - behind(magne...  31.7 us
    all_to_all x6, starting transfers between devices, all_by_exchange(): pieces = lax.all_to_all(pieces, axis, split_axis=0, concat_axis=0)  30.9 us
    ppermute x12, starting transfers between devices, passed_along(): return lax.ppermute(block, axis, route)  24.9 us
    add x6, other arithmetic, advance(): gradient_sum + (electric[0][0] * electric[0][1] + electric[1][0] * electr...  19.9 us
  transfers between devices with their start and end apart: 31, of which 19 were waited for; matrix products, arithmetic and copies ran while one was open for 3% of the time, Pallas kernels for 0%

profile of v1, /device:TPU:1, one launch (start us, length us, event | category | flops | bytes accessed | tf_op | source)
XLA Modules:
  0.0 993.4 jit_solution(13162309904667280901)
XLA Ops:
  14.8 826.8 %while.35 = (s32[]{:T(128)}, f32[2,4,256,256]{3,2,1,0:T(8,128)S(1)}, f32[2,4,256,256]{3,2,1,0:T(8,128)}, f32[2,4,256,256]{3,2,1,0:T(8,128)}, f32[2,4,256,256]{3,...) while((s32[]{:T(128)}, ...), condition=%wide.region_3.0_spmd.clone.clone, body=%wide.region_2.0_spmd.clone.clone.sunk | while | flops 25982984 | bytes 270941312 | solution.py:162
  20.4 23.2 %collective-permute-done = f32[2,2,256,256]{3,2,1,0:T(8,128)S(1)} collective-permute-done((f32[2,2,256,256]{3,2,1,0:T(8,128)S(1)}, f32[2,2,256,256]{3,2,1,0:T(8,128)S(1)}, u32[]{:S(2)}, u32[]{:S(2)}) %collective-permute-start) | collective-permute-done | bytes 1048608 | tf_op jit(solution)/shard_map/while/body/eval_jaxpr/ppermute | solution.py:33
  48.2 5.4 collective-permute-start.1
  56.7 17.1 %collective-permute-done.2 = f32[1,256]{1,0:T(1,128)S(1)} collective-permute-done((f32[1,256]{1,0:T(1,128)S(1)}, f32[1,256]{1,0:T(1,128)S(1)}, u32[]{:S(2)}, u32[]{:S(2)}) %collective-permute-start.2) | collective-permute-done | bytes 1056 | tf_op jit(solution)/shard_map/while/body/eval_jaxpr/ppermute | solution.py:24
  75.7 11.5 %all-to-all-start = ((f32[32,8,256]{2,1,0:T(8,128)}), f32[32,8,256]{2,1,0:T(8,128)S(1)}, u32[]{:S(2)}, u32[]{:S(2)}) async-start(f32[32,8,256]{2,1,0:T(8,128)} %stack.9), calls=%async_computation | async-start | bytes 524288 | tf_op jit(solution)/shard_map/while/body/eval_jaxpr/all_to_all | solution.py:13
  87.9 73.8 %all_gather.13 = f32[256,256]{1,0:T(8,128)} all-gather(f32[8,256]{1,0:T(8,128)S(1)} %get-tuple-element.676), channel_id=1, replica_groups=mesh['slab'=32,'run'=4] {'slab'}, dimensions={0}, use_global_device_ids=true | all-gather | bytes 270336 | tf_op jit(solution)/shard_map/while/body/eval_jaxpr/all_gather | solution.py:124
  167.3 5.3 fusion.43
  180.5 12.4 %collective-permute-done = f32[2,2,256,256]{3,2,1,0:T(8,128)S(1)} collective-permute-done((f32[2,2,256,256]{3,2,1,0:T(8,128)S(1)}, f32[2,2,256,256]{3,2,1,0:T(8,128)S(1)}, u32[]{:S(2)}, u32[]{:S(2)}) %collective-permute-start) | collective-permute-done | bytes 1048608 | tf_op jit(solution)/shard_map/while/body/eval_jaxpr/ppermute | solution.py:33
  202.7 8.3 collective-permute-done.2
  211.0 11.1 %collective-permute-done.3 = f32[1,256]{1,0:T(1,128)S(1)} collective-permute-done((f32[1,256]{1,0:T(1,128)S(1)}, f32[1,256]{1,0:T(1,128)S(1)}, u32[]{:S(2)}, u32[]{:S(2)}) %collective-permute-start.3) | collective-permute-done | bytes 1056 | tf_op jit(solution)/shard_map/while/body/eval_jaxpr/ppermute | solution.py:25
  222.9 3.9 all-to-all-start
  227.4 74.3 %all_gather.13 = f32[256,256]{1,0:T(8,128)} all-gather(f32[8,256]{1,0:T(8,128)S(1)} %get-tuple-element.676), channel_id=1, replica_groups=mesh['slab'=32,'run'=4] {'slab'}, dimensions={0}, use_global_device_ids=true | all-gather | bytes 270336 | tf_op jit(solution)/shard_map/while/body/eval_jaxpr/all_gather | solution.py:124
  307.3 5.3 fusion.43
  321.8 13.0 %collective-permute-done = f32[2,2,256,256]{3,2,1,0:T(8,128)S(1)} collective-permute-done((f32[2,2,256,256]{3,2,1,0:T(8,128)S(1)}, f32[2,2,256,256]{3,2,1,0:T(8,128)S(1)}, u32[]{:S(2)}, u32[]{:S(2)}) %collective-permute-start) | collective-permute-done | bytes 1048608 | tf_op jit(solution)/shard_map/while/body/eval_jaxpr/ppermute | solution.py:33
  344.5 8.3 collective-permute-done.2
  353.8 3.9 all-to-all-start
  358.2 74.4 %all_gather.13 = f32[256,256]{1,0:T(8,128)} all-gather(f32[8,256]{1,0:T(8,128)S(1)} %get-tuple-element.676), channel_id=1, replica_groups=mesh['slab'=32,'run'=4] {'slab'}, dimensions={0}, use_global_device_ids=true | all-gather | bytes 270336 | tf_op jit(solution)/shard_map/while/body/eval_jaxpr/all_gather | solution.py:124
  438.4 5.3 fusion.43
  452.9 13.1 %collective-permute-done = f32[2,2,256,256]{3,2,1,0:T(8,128)S(1)} collective-permute-done((f32[2,2,256,256]{3,2,1,0:T(8,128)S(1)}, f32[2,2,256,256]{3,2,1,0:T(8,128)S(1)}, u32[]{:S(2)}, u32[]{:S(2)}) %collective-permute-start) | collective-permute-done | bytes 1048608 | tf_op jit(solution)/shard_map/while/body/eval_jaxpr/ppermute | solution.py:33
  475.7 8.6 collective-permute-done.2
  485.6 3.9 all-to-all-start
  490.1 74.3 %all_gather.13 = f32[256,256]{1,0:T(8,128)} all-gather(f32[8,256]{1,0:T(8,128)S(1)} %get-tuple-element.676), channel_id=1, replica_groups=mesh['slab'=32,'run'=4] {'slab'}, dimensions={0}, use_global_device_ids=true | all-gather | bytes 270336 | tf_op jit(solution)/shard_map/while/body/eval_jaxpr/all_gather | solution.py:124
  570.1 5.3 fusion.43
  584.6 12.7 %collective-permute-done = f32[2,2,256,256]{3,2,1,0:T(8,128)S(1)} collective-permute-done((f32[2,2,256,256]{3,2,1,0:T(8,128)S(1)}, f32[2,2,256,256]{3,2,1,0:T(8,128)S(1)}, u32[]{:S(2)}, u32[]{:S(2)}) %collective-permute-start) | collective-permute-done | bytes 1048608 | tf_op jit(solution)/shard_map/while/body/eval_jaxpr/ppermute | solution.py:33
  607.2 8.7 collective-permute-done.2
  621.5 74.2 %all_gather.13 = f32[256,256]{1,0:T(8,128)} all-gather(f32[8,256]{1,0:T(8,128)S(1)} %get-tuple-element.676), channel_id=1, replica_groups=mesh['slab'=32,'run'=4] {'slab'}, dimensions={0}, use_global_device_ids=true | all-gather | bytes 270336 | tf_op jit(solution)/shard_map/while/body/eval_jaxpr/all_gather | solution.py:124
  701.4 5.3 fusion.43
  715.9 13.3 %collective-permute-done = f32[2,2,256,256]{3,2,1,0:T(8,128)S(1)} collective-permute-done((f32[2,2,256,256]{3,2,1,0:T(8,128)S(1)}, f32[2,2,256,256]{3,2,1,0:T(8,128)S(1)}, u32[]{:S(2)}, u32[]{:S(2)}) %collective-permute-start) | collective-permute-done | bytes 1048608 | tf_op jit(solution)/shard_map/while/body/eval_jaxpr/ppermute | solution.py:33
  738.9 8.7 collective-permute-done.2
  753.0 73.9 %all_gather.13 = f32[256,256]{1,0:T(8,128)} all-gather(f32[8,256]{1,0:T(8,128)S(1)} %get-tuple-element.676), channel_id=1, replica_groups=mesh['slab'=32,'run'=4] {'slab'}, dimensions={0}, use_global_device_ids=true | all-gather | bytes 270336 | tf_op jit(solution)/shard_map/while/body/eval_jaxpr/all_gather | solution.py:124
  832.6 5.3 fusion.43
  843.9 140.4 %all-reduce.13.cloned.1.call-done = f32[4,256,256]{2,1,0:T(8,128)} async-done(((f32[4,256,256]{2,1,0:T(8,128)}), f32[4,256,256]{2,1,0:T(8,128)}) %all-reduce.13.cloned.1.call-update) | async-done | bytes 1048592 | tf_op jit(solution)/shard_map/psum | solution.py:168
  (492 shorter events, 171.3 us)
Async XLA Ops:
  7.2 977.1 %all-reduce.13.cloned.1.call-start = ((), (), s32[]{:S(2)}) async-start(), calls=%async_computation.1 | async-start | bytes 2097152 | tf_op jit(solution)/shard_map/psum | solution.py:168
  14.8 60.2 %copy-start.18 = (f32[8,256]{1,0:T(8,128)}, f32[8,256]{1,0:T(8,128)S(1)}, u32[]{:S(2)}) copy-start(f32[8,256]{1,0:T(8,128)S(1)} %get-tuple-element.736) | copy-start | bytes 24580 | tf_op jit(solution)/shard_map/while
  17.2 26.3 %collective-permute-start = (f32[2,2,256,256]{3,2,1,0:T(8,128)S(1)}, f32[2,2,256,256]{3,2,1,0:T(8,128)S(1)}, u32[]{:S(2)}, u32[]{:S(2)}) collective-permute-start(f32[2,2,256,256]{3,2,1,0:T(8,128)S(1)} %pad_maximum_fusion.6), channel_id=1, source_target_pairs={{4,0},{8,4},{12,8},{16,12},{20,16},{24,20},{28,24},{32,28},{36,32}... | collective-permute-start | bytes 3145736 | tf_op jit(solution)/shard_map/while/body/eval_jaxpr/ppermute | solution.py:33
  48.2 116.6 %collective-permute-start.1 = (f32[2,2,256,256]{3,2,1,0:T(8,128)}, f32[2,2,256,256]{3,2,1,0:T(8,128)}, u32[]{:S(2)}, u32[]{:S(2)}) collective-permute-start(f32[2,2,256,256]{3,2,1,0:T(8,128)} %pad_maximum_fusion.7), channel_id=1, source_target_pairs={{0,4},{4,8},{8,12},{12,16},{16,20},{20,24},{24,28},{28,32},{32,36}... | collective-permute-start | bytes 3145736 | tf_op jit(solution)/shard_map/while/body/eval_jaxpr/ppermute | solution.py:33
  53.6 20.2 %collective-permute-start.2 = (f32[1,256]{1,0:T(1,128)S(1)}, f32[1,256]{1,0:T(1,128)S(1)}, u32[]{:S(2)}, u32[]{:S(2)}) collective-permute-start(f32[1,256]{1,0:T(1,128)S(1)} %get-tuple-element.673), channel_id=1, source_target_pairs={{0,4},{4,8},{8,12},{12,16},{16,20},{20,24},{24,28},{28,32},{32,36}... | collective-permute-start | bytes 3080 | tf_op jit(solution)/shard_map/while/body/eval_jaxpr/ppermute | solution.py:24
  55.3 19.6 %collective-permute-start.3 = (f32[1,256]{1,0:T(1,128)S(1)}, f32[1,256]{1,0:T(1,128)S(1)}, u32[]{:S(2)}, u32[]{:S(2)}) collective-permute-start(f32[1,256]{1,0:T(1,128)S(1)} %get-tuple-element.674), channel_id=1, source_target_pairs={{4,0},{8,4},{12,8},{16,12},{20,16},{24,20},{28,24},{32,28},{36,32}... | collective-permute-start | bytes 3080 | tf_op jit(solution)/shard_map/while/body/eval_jaxpr/ppermute | solution.py:25
  75.7 85.9 %all-to-all-start = ((f32[32,8,256]{2,1,0:T(8,128)}), f32[32,8,256]{2,1,0:T(8,128)S(1)}, u32[]{:S(2)}, u32[]{:S(2)}) async-start(f32[32,8,256]{2,1,0:T(8,128)} %stack.9), calls=%async_computation | async-start | bytes 524288 | tf_op jit(solution)/shard_map/while/body/eval_jaxpr/all_to_all | solution.py:13
  177.3 15.5 %collective-permute-start = (f32[2,2,256,256]{3,2,1,0:T(8,128)S(1)}, f32[2,2,256,256]{3,2,1,0:T(8,128)S(1)}, u32[]{:S(2)}, u32[]{:S(2)}) collective-permute-start(f32[2,2,256,256]{3,2,1,0:T(8,128)S(1)} %pad_maximum_fusion.6), channel_id=1, source_target_pairs={{4,0},{8,4},{12,8},{16,12},{20,16},{24,20},{28,24},{32,28},{36,32}... | collective-permute-start | bytes 3145736 | tf_op jit(solution)/shard_map/while/body/eval_jaxpr/ppermute | solution.py:33
  197.5 107.2 %collective-permute-start.1 = (f32[2,2,256,256]{3,2,1,0:T(8,128)}, f32[2,2,256,256]{3,2,1,0:T(8,128)}, u32[]{:S(2)}, u32[]{:S(2)}) collective-permute-start(f32[2,2,256,256]{3,2,1,0:T(8,128)} %pad_maximum_fusion.7), channel_id=1, source_target_pairs={{0,4},{4,8},{8,12},{12,16},{16,20},{20,24},{24,28},{28,32},{32,36}... | collective-permute-start | bytes 3145736 | tf_op jit(solution)/shard_map/while/body/eval_jaxpr/ppermute | solution.py:33
  200.0 11.0 %collective-permute-start.2 = (f32[1,256]{1,0:T(1,128)S(1)}, f32[1,256]{1,0:T(1,128)S(1)}, u32[]{:S(2)}, u32[]{:S(2)}) collective-permute-start(f32[1,256]{1,0:T(1,128)S(1)} %get-tuple-element.673), channel_id=1, source_target_pairs={{0,4},{4,8},{8,12},{12,16},{16,20},{20,24},{24,28},{28,32},{32,36}... | collective-permute-start | bytes 3080 | tf_op jit(solution)/shard_map/while/body/eval_jaxpr/ppermute | solution.py:24
  201.3 20.8 %collective-permute-start.3 = (f32[1,256]{1,0:T(1,128)S(1)}, f32[1,256]{1,0:T(1,128)S(1)}, u32[]{:S(2)}, u32[]{:S(2)}) collective-permute-start(f32[1,256]{1,0:T(1,128)S(1)} %get-tuple-element.674), channel_id=1, source_target_pairs={{4,0},{8,4},{12,8},{16,12},{20,16},{24,20},{28,24},{32,28},{36,32}... | collective-permute-start | bytes 3080 | tf_op jit(solution)/shard_map/while/body/eval_jaxpr/ppermute | solution.py:25
  222.9 78.7 %all-to-all-start = ((f32[32,8,256]{2,1,0:T(8,128)}), f32[32,8,256]{2,1,0:T(8,128)S(1)}, u32[]{:S(2)}, u32[]{:S(2)}) async-start(f32[32,8,256]{2,1,0:T(8,128)} %stack.9), calls=%async_computation | async-start | bytes 524288 | tf_op jit(solution)/shard_map/while/body/eval_jaxpr/all_to_all | solution.py:13
  318.7 16.2 %collective-permute-start = (f32[2,2,256,256]{3,2,1,0:T(8,128)S(1)}, f32[2,2,256,256]{3,2,1,0:T(8,128)S(1)}, u32[]{:S(2)}, u32[]{:S(2)}) collective-permute-start(f32[2,2,256,256]{3,2,1,0:T(8,128)S(1)} %pad_maximum_fusion.6), channel_id=1, source_target_pairs={{4,0},{8,4},{12,8},{16,12},{20,16},{24,20},{28,24},{32,28},{36,32}... | collective-permute-start | bytes 3145736 | tf_op jit(solution)/shard_map/while/body/eval_jaxpr/ppermute | solution.py:33
  339.5 96.3 %collective-permute-start.1 = (f32[2,2,256,256]{3,2,1,0:T(8,128)}, f32[2,2,256,256]{3,2,1,0:T(8,128)}, u32[]{:S(2)}, u32[]{:S(2)}) collective-permute-start(f32[2,2,256,256]{3,2,1,0:T(8,128)} %pad_maximum_fusion.7), channel_id=1, source_target_pairs={{0,4},{4,8},{8,12},{12,16},{16,20},{20,24},{24,28},{28,32},{32,36}... | collective-permute-start | bytes 3145736 | tf_op jit(solution)/shard_map/while/body/eval_jaxpr/ppermute | solution.py:33
  341.8 11.0 %collective-permute-start.2 = (f32[1,256]{1,0:T(1,128)S(1)}, f32[1,256]{1,0:T(1,128)S(1)}, u32[]{:S(2)}, u32[]{:S(2)}) collective-permute-start(f32[1,256]{1,0:T(1,128)S(1)} %get-tuple-element.673), channel_id=1, source_target_pairs={{0,4},{4,8},{8,12},{12,16},{16,20},{20,24},{24,28},{28,32},{32,36}... | collective-permute-start | bytes 3080 | tf_op jit(solution)/shard_map/while/body/eval_jaxpr/ppermute | solution.py:24
  343.1 9.9 collective-permute-start.3
  353.8 78.9 %all-to-all-start = ((f32[32,8,256]{2,1,0:T(8,128)}), f32[32,8,256]{2,1,0:T(8,128)S(1)}, u32[]{:S(2)}, u32[]{:S(2)}) async-start(f32[32,8,256]{2,1,0:T(8,128)} %stack.9), calls=%async_computation | async-start | bytes 524288 | tf_op jit(solution)/shard_map/while/body/eval_jaxpr/all_to_all | solution.py:13
  449.7 16.3 %collective-permute-start = (f32[2,2,256,256]{3,2,1,0:T(8,128)S(1)}, f32[2,2,256,256]{3,2,1,0:T(8,128)S(1)}, u32[]{:S(2)}, u32[]{:S(2)}) collective-permute-start(f32[2,2,256,256]{3,2,1,0:T(8,128)S(1)} %pad_maximum_fusion.6), channel_id=1, source_target_pairs={{4,0},{8,4},{12,8},{16,12},{20,16},{24,20},{28,24},{32,28},{36,32}... | collective-permute-start | bytes 3145736 | tf_op jit(solution)/shard_map/while/body/eval_jaxpr/ppermute | solution.py:33
  470.7 96.9 %collective-permute-start.1 = (f32[2,2,256,256]{3,2,1,0:T(8,128)}, f32[2,2,256,256]{3,2,1,0:T(8,128)}, u32[]{:S(2)}, u32[]{:S(2)}) collective-permute-start(f32[2,2,256,256]{3,2,1,0:T(8,128)} %pad_maximum_fusion.7), channel_id=1, source_target_pairs={{0,4},{4,8},{8,12},{12,16},{16,20},{20,24},{24,28},{28,32},{32,36}... | collective-permute-start | bytes 3145736 | tf_op jit(solution)/shard_map/while/body/eval_jaxpr/ppermute | solution.py:33
  472.9 11.3 %collective-permute-start.2 = (f32[1,256]{1,0:T(1,128)S(1)}, f32[1,256]{1,0:T(1,128)S(1)}, u32[]{:S(2)}, u32[]{:S(2)}) collective-permute-start(f32[1,256]{1,0:T(1,128)S(1)} %get-tuple-element.673), channel_id=1, source_target_pairs={{0,4},{4,8},{8,12},{12,16},{16,20},{20,24},{24,28},{28,32},{32,36}... | collective-permute-start | bytes 3080 | tf_op jit(solution)/shard_map/while/body/eval_jaxpr/ppermute | solution.py:24
  474.2 10.6 %collective-permute-start.3 = (f32[1,256]{1,0:T(1,128)S(1)}, f32[1,256]{1,0:T(1,128)S(1)}, u32[]{:S(2)}, u32[]{:S(2)}) collective-permute-start(f32[1,256]{1,0:T(1,128)S(1)} %get-tuple-element.674), channel_id=1, source_target_pairs={{4,0},{8,4},{12,8},{16,12},{20,16},{24,20},{28,24},{32,28},{36,32}... | collective-permute-start | bytes 3080 | tf_op jit(solution)/shard_map/while/body/eval_jaxpr/ppermute | solution.py:25
  485.6 78.8 %all-to-all-start = ((f32[32,8,256]{2,1,0:T(8,128)}), f32[32,8,256]{2,1,0:T(8,128)S(1)}, u32[]{:S(2)}, u32[]{:S(2)}) async-start(f32[32,8,256]{2,1,0:T(8,128)} %stack.9), calls=%async_computation | async-start | bytes 524288 | tf_op jit(solution)/shard_map/while/body/eval_jaxpr/all_to_all | solution.py:13
  581.4 15.9 %collective-permute-start = (f32[2,2,256,256]{3,2,1,0:T(8,128)S(1)}, f32[2,2,256,256]{3,2,1,0:T(8,128)S(1)}, u32[]{:S(2)}, u32[]{:S(2)}) collective-permute-start(f32[2,2,256,256]{3,2,1,0:T(8,128)S(1)} %pad_maximum_fusion.6), channel_id=1, source_target_pairs={{4,0},{8,4},{12,8},{16,12},{20,16},{24,20},{28,24},{32,28},{36,32}... | collective-permute-start | bytes 3145736 | tf_op jit(solution)/shard_map/while/body/eval_jaxpr/ppermute | solution.py:33
  602.0 96.9 %collective-permute-start.1 = (f32[2,2,256,256]{3,2,1,0:T(8,128)}, f32[2,2,256,256]{3,2,1,0:T(8,128)}, u32[]{:S(2)}, u32[]{:S(2)}) collective-permute-start(f32[2,2,256,256]{3,2,1,0:T(8,128)} %pad_maximum_fusion.7), channel_id=1, source_target_pairs={{0,4},{4,8},{8,12},{12,16},{16,20},{20,24},{24,28},{28,32},{32,36}... | collective-permute-start | bytes 3145736 | tf_op jit(solution)/shard_map/while/body/eval_jaxpr/ppermute | solution.py:33
  604.4 11.4 %collective-permute-start.2 = (f32[1,256]{1,0:T(1,128)S(1)}, f32[1,256]{1,0:T(1,128)S(1)}, u32[]{:S(2)}, u32[]{:S(2)}) collective-permute-start(f32[1,256]{1,0:T(1,128)S(1)} %get-tuple-element.673), channel_id=1, source_target_pairs={{0,4},{4,8},{8,12},{12,16},{16,20},{20,24},{24,28},{28,32},{32,36}... | collective-permute-start | bytes 3080 | tf_op jit(solution)/shard_map/while/body/eval_jaxpr/ppermute | solution.py:24
  605.7 10.5 %collective-permute-start.3 = (f32[1,256]{1,0:T(1,128)S(1)}, f32[1,256]{1,0:T(1,128)S(1)}, u32[]{:S(2)}, u32[]{:S(2)}) collective-permute-start(f32[1,256]{1,0:T(1,128)S(1)} %get-tuple-element.674), channel_id=1, source_target_pairs={{4,0},{8,4},{12,8},{16,12},{20,16},{24,20},{28,24},{32,28},{36,32}... | collective-permute-start | bytes 3080 | tf_op jit(solution)/shard_map/while/body/eval_jaxpr/ppermute | solution.py:25
  617.0 78.7 %all-to-all-start = ((f32[32,8,256]{2,1,0:T(8,128)}), f32[32,8,256]{2,1,0:T(8,128)S(1)}, u32[]{:S(2)}, u32[]{:S(2)}) async-start(f32[32,8,256]{2,1,0:T(8,128)} %stack.9), calls=%async_computation | async-start | bytes 524288 | tf_op jit(solution)/shard_map/while/body/eval_jaxpr/all_to_all | solution.py:13
  712.8 16.5 %collective-permute-start = (f32[2,2,256,256]{3,2,1,0:T(8,128)S(1)}, f32[2,2,256,256]{3,2,1,0:T(8,128)S(1)}, u32[]{:S(2)}, u32[]{:S(2)}) collective-permute-start(f32[2,2,256,256]{3,2,1,0:T(8,128)S(1)} %pad_maximum_fusion.6), channel_id=1, source_target_pairs={{4,0},{8,4},{12,8},{16,12},{20,16},{24,20},{28,24},{32,28},{36,32}... | collective-permute-start | bytes 3145736 | tf_op jit(solution)/shard_map/while/body/eval_jaxpr/ppermute | solution.py:33
  733.9 96.2 %collective-permute-start.1 = (f32[2,2,256,256]{3,2,1,0:T(8,128)}, f32[2,2,256,256]{3,2,1,0:T(8,128)}, u32[]{:S(2)}, u32[]{:S(2)}) collective-permute-start(f32[2,2,256,256]{3,2,1,0:T(8,128)} %pad_maximum_fusion.7), channel_id=1, source_target_pairs={{0,4},{4,8},{8,12},{12,16},{16,20},{20,24},{24,28},{28,32},{32,36}... | collective-permute-start | bytes 3145736 | tf_op jit(solution)/shard_map/while/body/eval_jaxpr/ppermute | solution.py:33
  736.2 11.4 %collective-permute-start.2 = (f32[1,256]{1,0:T(1,128)S(1)}, f32[1,256]{1,0:T(1,128)S(1)}, u32[]{:S(2)}, u32[]{:S(2)}) collective-permute-start(f32[1,256]{1,0:T(1,128)S(1)} %get-tuple-element.673), channel_id=1, source_target_pairs={{0,4},{4,8},{8,12},{12,16},{16,20},{20,24},{24,28},{28,32},{32,36}... | collective-permute-start | bytes 3080 | tf_op jit(solution)/shard_map/while/body/eval_jaxpr/ppermute | solution.py:24
  737.5 10.2 %collective-permute-start.3 = (f32[1,256]{1,0:T(1,128)S(1)}, f32[1,256]{1,0:T(1,128)S(1)}, u32[]{:S(2)}, u32[]{:S(2)}) collective-permute-start(f32[1,256]{1,0:T(1,128)S(1)} %get-tuple-element.674), channel_id=1, source_target_pairs={{4,0},{8,4},{12,8},{16,12},{20,16},{24,20},{28,24},{32,28},{36,32}... | collective-permute-start | bytes 3080 | tf_op jit(solution)/shard_map/while/body/eval_jaxpr/ppermute | solution.py:25
  748.5 78.4 %all-to-all-start = ((f32[32,8,256]{2,1,0:T(8,128)}), f32[32,8,256]{2,1,0:T(8,128)S(1)}, u32[]{:S(2)}, u32[]{:S(2)}) async-start(f32[32,8,256]{2,1,0:T(8,128)} %stack.9), calls=%async_computation | async-start | bytes 524288 | tf_op jit(solution)/shard_map/while/body/eval_jaxpr/all_to_all | solution.py:13
  (143 other events, 1196.0 us)
Sparse Core Ops, SparseCore 0:
  841.7 142.5 all-reduce.12
